TPU v7x, 32 devices: a whole 2x2x4 slice. The times are simulated.
32 devices in a mesh: seq: 16 (over z, x, core), head: 2 (over y).
Axes of the slice: x: 2, y: 2, z: 4, core: 2. Of those that a mesh axis runs over, the one named last changes fastest.
Arguments:
- queries: bfloat16 [16384, 4096], P('seq', 'head'), may hold values from -0.5 to 0.5
- key_rows: bfloat16 [16384, 4096], P('seq', 'head'), may hold values from -6 to 6
- value_rows: bfloat16 [16384, 4096], P('seq', 'head'), may hold values from -6 to 6
- decay_rates: float32 [32], P('head'), as said below
- out_gain: float32 [4096], P('head'), may hold values from 0.5 to 1.5
Outputs:
- attended: bfloat16 [16384, 4096], P('seq', 'head')
Inputs may be any that keep to these rules, and one draw needn't show every extreme that they name: `decay_rates`: positive per-head decay rates.
All inputs are finite; a program needn't handle non-finite values.
Results may differ from a plain program's by a relative error of at most 0.0054.
Values sent between devices are 32-bit elements; how exact they have to be, the bound alone decides.
A program may use at most 128 MiB of HBM per device.

v0:
```python
import functools

import jax
import jax.numpy as jnp
from jax import lax
from jax.experimental import pallas as pl
from jax.experimental.pallas import tpu as pltpu
from jax.sharding import PartitionSpec as P

E = 128
BLOCK = 256
EPSILON = 1e-06
GROUP = 4
CUTS = 1
PIECE = E // CUTS
F32 = jnp.float32
BF16 = jnp.bfloat16


def dot(a, b, contract):
    return lax.dot_general(a, b, ((contract[:1], contract[1:]), ((), ())), preferred_element_type=F32)


def kernel(
    runs, ways,
    q_hbm, k_hbm, v_hbm, rates_hbm, mix, sums_ref,
    rates, q_buf, k_buf, v_buf, local, acc, entering,
    s_loc, s_oth, c_tot, c_oth, p_in, p_out, e_mine, e_send, e_oth, ss_loc, ss_in,
    r_sem, q_sem, k_sem, v_sem, s_ss, s_rs, c_ss, c_rs, p_ss, p_rs, e_ss, e_rs, n_ss, n_rs,
):
    heads, length = q_buf.shape[0], q_buf.shape[1]
    half = heads // 2
    blocks = length // BLOCK
    groups = runs // GROUP
    me = lax.axis_index("seq")
    way = lax.axis_index("head")
    core = lax.rem(me, 2)
    x = lax.rem(me // 2, 2)
    z = me // GROUP
    core_peer = me + 1 - 2 * core
    x_peer = me + 2 - 4 * x
    own0 = core * half
    oth0 = (1 - core) * half
    core_f = core.astype(F32)
    x_f = x.astype(F32)

    def load(hbm, buf, sem, h):
        return pltpu.make_async_copy(hbm.at[:, pl.ds(pl.multiple_of(h * E, E), E)], buf.at[h], sem.at[h])

    def remote(src, dst, ss, rs, seq, head):
        return pltpu.make_async_remote_copy(
            src_ref=src, dst_ref=dst, send_sem=ss, recv_sem=rs,
            device_id={"seq": seq, "head": head}, device_id_type=pl.DeviceIdType.MESH,
        )

    def state_copy(k):
        return remote(s_loc.at[oth0 + k], s_oth.at[k], s_ss.at[k], s_rs.at[k], core_peer, way)

    def chip_copy(k):
        return remote(c_tot.at[k], c_oth.at[k], c_ss.at[k], c_rs.at[k], x_peer, way)

    def chain_copy(k):
        up = lax.rem(me + GROUP, runs)
        return remote(p_out.at[k], p_in.at[k], p_ss.at[k], p_rs.at[k], up, way)

    def carry_copy(k):
        return remote(e_send.at[k], e_oth.at[k], e_ss.at[k], e_rs.at[k], core_peer, way)

    def norm_copy(d):
        return remote(ss_loc, ss_in.at[d - 1], n_ss.at[d - 1], n_rs.at[d - 1], me, lax.rem(way + d, ways))

    def start_states(k, c):
        for h in (own0 + k, oth0 + k):
            load(k_hbm, k_buf, k_sem, h).start()
            load(v_hbm, v_buf, v_sem, h).start()
        return c

    def start_queries(k, c):
        for h in (own0 + k, oth0 + k):
            load(q_hbm, q_buf, q_sem, h).start()
        return c

    rates_copy = pltpu.make_async_copy(rates_hbm, rates, r_sem)
    rates_copy.start()
    lax.fori_loop(0, half, start_states, 0)
    lax.fori_loop(0, half, start_queries, 0)

    barrier = pltpu.get_barrier_semaphore()

    def greet(seq, head):
        pl.semaphore_signal(
            barrier, inc=1, device_id={"seq": seq, "head": head}, device_id_type=pl.DeviceIdType.MESH
        )

    greet(core_peer, way)
    greet(x_peer, way)
    for d in range(1, ways):
        greet(me, lax.rem(way + d, ways))

    @pl.when(z > 0)
    def _():
        greet(me - GROUP, way)

    @pl.when(z < groups - 1)
    def _():
        greet(me + GROUP, way)

    @pl.when(z == 0)
    def _():
        p_in[...] = jnp.zeros_like(p_in)

    acc[...] = jnp.zeros_like(acc)
    rates_copy.wait()

    def power(rate, steps):
        return jnp.exp(jnp.full((1, E), -rate * steps, F32))

    row = lax.broadcasted_iota(jnp.int32, (8, E), 0).astype(F32)

    def rising(rate):
        column = jnp.exp(-rate * (row + 1.0))
        while column.shape[0] < BLOCK:
            column = jnp.concatenate([column, column * power(rate, float(column.shape[0]))], axis=0)
        return column

    def falling(rate):
        column = jnp.exp(-rate * (7.0 - row))
        while column.shape[0] < BLOCK:
            column = jnp.concatenate([column * power(rate, float(column.shape[0])), column], axis=0)
        return column


    def local_states(k):
        pair = (oth0 + k, own0 + k)
        for h in pair:
            load(k_hbm, k_buf, k_sem, h).wait()
            load(v_hbm, v_buf, v_sem, h).wait()
        whole = [power(rates[h], float(BLOCK)) for h in pair]
        scale = [falling(rates[h]) for h in pair]
        state = [None, None]
        for b in range(blocks):
            rows = pl.ds(b * BLOCK, BLOCK)
            for n, h in enumerate(pair):
                scaled = (k_buf[h, rows, :].astype(F32) * scale[n]).astype(BF16)
                part = dot(scaled, v_buf[h, rows, :], (0, 0))
                state[n] = part if b == 0 else state[n] * whole[n] + part
                if b < blocks - 1:
                    entering[h, b] = state[n]
                else:
                    s_loc[h] = state[n]

    def chip_total(k):
        rate = rates[own0 + k]
        state_copy(k).wait_recv()
        mine = power(rate, length * (1.0 - core_f))
        other = power(rate, length * core_f)
        for p in range(CUTS):
            rows = pl.ds(p * PIECE, PIECE)
            c_tot[k * CUTS + p] = mine * s_loc[own0 + k, rows, :] + other * s_oth[k, rows, :]
            chip_copy(k * CUTS + p).start()

    def state_step(k, c):
        local_states(k)
        state_copy(k).start()
        chip_total(k - 1)
        return c

    local_states(0)
    pl.semaphore_wait(barrier, 2 + (ways - 1) + jnp.minimum(z, 1) + jnp.minimum(groups - 1 - z, 1))
    state_copy(0).start()
    lax.fori_loop(1, half, state_step, 0)
    chip_total(half - 1)

    small = E
    down = lax.broadcasted_iota(jnp.int32, (small, small), 0) - lax.broadcasted_iota(jnp.int32, (small, small), 1)
    down_f = down.astype(F32)
    left = (small - 1) - lax.broadcasted_iota(jnp.int32, (1, small), 1).astype(F32)
    blank = jnp.zeros((small, small), BF16)

    def attend(k):
        pair = (own0 + k, oth0 + k)
        for h in pair:
            load(q_hbm, q_buf, q_sem, h).wait()
        near = [jnp.where(down >= 0, jnp.exp(-rates[h] * jnp.maximum(down_f, 0.0)), 0.0) for h in pair]
        far = [rising(rates[h])[:small] * jnp.exp(-rates[h] * left) for h in pair]
        units = [(n, b) for n in range(2) for b in range(blocks)]

        def score(unit):
            rows = pl.ds(unit[1] * BLOCK, BLOCK)
            return dot(q_buf[pair[unit[0]], rows, :], k_buf[pair[unit[0]], rows, :], (1, 1))

        ahead = score(units[0])
        for at, (n, b) in enumerate(units):
            scores = ahead
            if at + 1 < len(units):
                ahead = score(units[at + 1])
            vals = v_buf[pair[n], pl.ds(b * BLOCK, BLOCK), :]
            top = jnp.concatenate([(scores[:small, :small] * near[n]).astype(BF16), blank], axis=1)
            low = jnp.concatenate(
                [(scores[small:, :small] * far[n]).astype(BF16), (scores[small:, small:] * near[n]).astype(BF16)],
                axis=1,
            )
            local[pair[n], pl.ds(b * BLOCK, BLOCK), :] = dot(jnp.concatenate([top, low], axis=0), vals, (1, 0))

    def chain(s):
        k = s // CUTS
        rows = pl.ds(pl.multiple_of(lax.rem(s, CUTS) * PIECE, PIECE), PIECE)
        rate = rates[own0 + k]
        chip_copy(s).wait_recv()

        @pl.when(z > 0)
        def _():
            chain_copy(s).wait_recv()

        before = p_in[s]
        other = c_oth[s]
        two = 2.0 * length

        @pl.when(z < groups - 1)
        def _():
            total = power(rate, two * (1.0 - x_f)) * c_tot[s] + power(rate, two * x_f) * other
            p_out[s] = power(rate, 2.0 * two) * before + total
            chain_copy(s).start()

        chip = power(rate, two * x_f) * before + x_f * other

        @pl.when(core == 0)
        def _():
            e_mine[s] = chip
            e_send[s] = power(rate, float(length)) * chip + s_loc[own0 + k, rows, :]

        @pl.when(core == 1)
        def _():
            e_mine[s] = power(rate, float(length)) * chip + s_oth[k, rows, :]
            e_send[s] = chip

        carry_copy(s).start()

    def finish(k):
        pair = (own0 + k, oth0 + k)
        for p in range(CUTS):
            carry_copy(k * CUTS + p).wait_recv()
        parts = pl.ds(k * CUTS, CUTS)
        carry = (e_mine[parts].reshape(E, E), e_oth[parts].reshape(E, E))
        scale = [rising(rates[h]) for h in pair]
        units = [(n, b) for b in range(blocks) for n in range(2)]

        def carried(unit):
            n, b = unit
            h = pair[n]
            state = carry[n]
            if b > 0:
                state = power(rates[h], float(b * BLOCK)) * state + entering[h, b - 1]
            return dot(q_buf[h, pl.ds(b * BLOCK, BLOCK), :], state.astype(BF16), (1, 0))

        ahead = carried(units[0])
        squares = None
        for at, (n, b) in enumerate(units):
            now = ahead
            if at + 1 < len(units):
                ahead = carried(units[at + 1])
            rows = pl.ds(b * BLOCK, BLOCK)
            mixed = local[pair[n], rows, :] + scale[n] * now
            mix[pair[n], rows, :] = mixed
            squares = mixed * mixed if n == 0 else squares + mixed * mixed
            if n == 1:
                acc[rows, :] += squares

    top_lag = half - 1
    lag = jnp.where(z == groups - 1, top_lag, jnp.minimum(z, top_lag))

    def step(i, c):
        @pl.when(i < half)
        def _():
            attend(i)

        def turn(n, c):
            k = 2 * (i - lag) + n
            here = jnp.logical_and(k >= 0, k < half)

            @pl.when(here)
            def _():
                chain(k * CUTS)

            j = 2 * (i - top_lag) + n - 1

            @pl.when(jnp.logical_and(j >= 0, j < half))
            def _():
                finish(j)

            @pl.when(here)
            def _():
                for p in range(1, CUTS):
                    chain(k * CUTS + p)

            return c

        return lax.fori_loop(0, 2, turn, c)

    lax.fori_loop(0, max(half, top_lag + (half + 1) // 2 + 1), step, 0)

    slabs = length // E
    for g in range(slabs):
        ss_loc[pl.ds(g, 1), :] = jnp.sum(acc[pl.ds(g * E, E), :].T, axis=0, keepdims=True)
    for d in range(1, ways):
        norm_copy(d).start()
    for d in range(1, ways):
        norm_copy(d).wait_recv()
    sums = ss_loc[...]
    for d in range(1, ways):
        sums = sums + ss_in[d - 1]
    sums_ref[...] = sums

    def drain(k, c):
        state_copy(k).wait_send()
        for p in range(CUTS):
            chip_copy(k * CUTS + p).wait_send()
            carry_copy(k * CUTS + p).wait_send()

        @pl.when(z < groups - 1)
        def _():
            for p in range(CUTS):
                chain_copy(k * CUTS + p).wait_send()

        return c

    lax.fori_loop(0, half, drain, 0)
    for d in range(1, ways):
        norm_copy(d).wait_send()


def normalise(width, mixed_ref, sums_ref, gain_hbm, out_hbm, gain, ready, gain_sem, out_sem):
    slabs = mixed_ref.shape[1] // E
    fetch = pltpu.make_async_copy(gain_hbm, gain, gain_sem)
    fetch.start()

    def put(t):
        rows = pl.ds(pl.multiple_of(t * E, E), E)
        return pltpu.make_async_copy(ready.at[rows], out_hbm.at[rows], out_sem.at[t])

    fetch.wait()

    def slab(t, c):
        inverse = jnp.broadcast_to(lax.rsqrt(sums_ref[pl.ds(t, 1), :] / width + EPSILON), (E, E)).T
        rows = pl.ds(pl.multiple_of(t * E, E), E)
        for h in range(mixed_ref.shape[0]):
            cols = pl.ds(h * E, E)
            ready[rows, cols] = (mixed_ref[h, rows, :] * inverse * gain[:, cols]).astype(BF16)
        put(t).start()
        return c

    lax.fori_loop(0, slabs, slab, 0)

    def drain(t, c):
        put(t).wait()
        return c

    lax.fori_loop(0, slabs, drain, 0)


def body(runs, ways, queries, key_rows, value_rows, decay_rates, out_gain):
    length, columns = queries.shape
    heads = decay_rates.shape[0]
    half = heads // 2
    blocks = length // BLOCK
    dma = pltpu.SemaphoreType.DMA
    states = [pltpu.VMEM((half, E, E), F32)]
    sems = [dma((half,))]
    fixed = [pltpu.with_memory_space_constraint(a, pltpu.HBM) for a in (queries, key_rows, value_rows, decay_rates)]
    gain = pltpu.with_memory_space_constraint(out_gain.reshape(1, columns), pltpu.HBM)
    sums_shape = (length // E, E)
    mixed, sums = pl.pallas_call(
        functools.partial(kernel, runs, ways),
        out_shape=(jax.ShapeDtypeStruct((heads, length, E), F32), jax.ShapeDtypeStruct(sums_shape, F32)),
        in_specs=[pl.BlockSpec(memory_space=pltpu.HBM)] * 4,
        out_specs=(pl.BlockSpec(memory_space=pltpu.VMEM),) * 2,
        scratch_shapes=[pltpu.SMEM((heads,), F32)]
        + [pltpu.VMEM((heads, length, E), BF16)] * 3
        + [
            pltpu.VMEM((heads, length, E), F32),
            pltpu.VMEM((length, E), F32),
            pltpu.VMEM((heads, blocks - 1, E, E), F32),
            pltpu.VMEM((heads, E, E), F32),
        ]
        + states
        + [pltpu.VMEM((half * CUTS, PIECE, E), F32)] * 7
        + [pltpu.VMEM(sums_shape, F32), pltpu.VMEM((max(ways - 1, 1),) + sums_shape, F32)]
        + [dma]
        + [dma((heads,))] * 3
        + sems * 2
        + [dma((half * CUTS,))] * 6
        + [dma((max(ways - 1, 1),))] * 2,
        compiler_params=pltpu.CompilerParams(
            collective_id=0, has_side_effects=True, vmem_limit_bytes=40 * 1024 * 1024
        ),
        cost_estimate=pl.CostEstimate(
            flops=12 * length * BLOCK * heads * E, bytes_accessed=8 * length * heads * E, transcendentals=0
        ),
    )(*fixed)
    return pl.pallas_call(
        functools.partial(normalise, float(heads * ways * E)),
        out_shape=jax.ShapeDtypeStruct(queries.shape, BF16),
        in_specs=[pl.BlockSpec(memory_space=pltpu.VMEM)] * 2 + [pl.BlockSpec(memory_space=pltpu.HBM)],
        out_specs=pl.BlockSpec(memory_space=pltpu.HBM),
        scratch_shapes=[
            pltpu.VMEM((1, columns), F32),
            pltpu.VMEM(queries.shape, BF16),
            dma,
            dma((length // E,)),
        ],
        compiler_params=pltpu.CompilerParams(vmem_limit_bytes=16 * 1024 * 1024),
        cost_estimate=pl.CostEstimate(
            flops=3 * length * columns, bytes_accessed=4 * length * columns, transcendentals=0
        ),
    )(mixed, sums, gain)


def solution(mesh):
    placed = (P("seq", "head"), P("seq", "head"), P("seq", "head"), P("head"), P("head"))
    return jax.shard_map(
        functools.partial(body, mesh.shape["seq"], mesh.shape["head"]),
        mesh=mesh, in_specs=placed, out_specs=P("seq", "head"), check_vma=False,
    )
```

profile of v0, /device:TPU:24, one launch (start us, length us, event | category | flops | bytes accessed | tf_op | source)
XLA Modules:
  0.0 35.2 jit_solution(7533969752446495833)
XLA Ops:
  0.0 32.0 %shard_map.55 = (f32[16,1024,128]{2,1,0:T(8,128)S(1)}, f32[8,128]{1,0:T(8,128)S(1)}) custom-call(bf16[1024,2048]{1,0:T(8,128)(2,1)} %q_hbm.1, bf16[1024,2048]{1,0:T(8,128)(2,1)} %k_hbm.1, bf16[1024,2048]{1,0:T(8,128)(2,1)} %v_hbm.1, f32[16]{0:T(128)} %rates_hbm.1), custom_call_target="tpu_custom_call" | custom-call | flops 6442450944 | bytes 16777216 | tf_op jit(solution)/shard_map/pallas_call | solution.py:372
  32.0 3.2 %shard_map.56 = bf16[1024,2048]{1,0:T(8,128)(2,1)} custom-call(f32[16,1024,128]{2,1,0:T(8,128)S(1)} %get-tuple-element.7.mixed_ref, f32[8,128]{1,0:T(8,128)S(1)} %get-tuple-element.8.sums_ref, f32[1,2048]{1,0:T(1,128)} %bitcast.1), custom_call_target="tpu_custom_call" | custom-call | flops 6291456 | bytes 8388608 | tf_op jit(solution)/shard_map/pallas_call | solution.py:400
where the time goes:
time: 35.6 us; the launch traced here: 35.2 us
  Pallas kernels  35.2 us (99%)
    pallas_call x1, Pallas kernels, body(): pl.pallas_call(functools.partial(kernel, runs, ways), out_shape=(jax.Shap...  32 us
    pallas_call x1, Pallas kernels, body(): pl.pallas_call(functools.partial(normalise, float(heads * ways * E)), out...  3.15 us

commit v1 on v0

--- a/solution.py
+++ b/solution.py
@@ -11,8 +11,6 @@
 BLOCK = 256
 EPSILON = 1e-06
 GROUP = 4
-CUTS = 1
-PIECE = E // CUTS
 F32 = jnp.float32
 BF16 = jnp.bfloat16
 
@@ -25,11 +23,12 @@
     runs, ways,
     q_hbm, k_hbm, v_hbm, rates_hbm, mix, sums_ref,
     rates, q_buf, k_buf, v_buf, local, acc, entering,
-    s_loc, s_oth, c_tot, c_oth, p_in, p_out, e_mine, e_send, e_oth, ss_loc, ss_in,
-    r_sem, q_sem, k_sem, v_sem, s_ss, s_rs, c_ss, c_rs, p_ss, p_rs, e_ss, e_rs, n_ss, n_rs,
+    s_loc, s_oth, c_tot, c_oth, p_in, p_out, g_out, g_in, e_mine, e_send, e_oth, ss_loc, ss_in,
+    r_sem, q_sem, k_sem, v_sem, s_ss, s_rs, c_ss, c_rs, p_ss, p_rs, g_ss, g_rs, e_ss, e_rs, n_ss, n_rs,
 ):
     heads, length = q_buf.shape[0], q_buf.shape[1]
     half = heads // 2
+    quarter = half // 2
     blocks = length // BLOCK
     groups = runs // GROUP
     me = lax.axis_index("seq")
@@ -56,12 +55,15 @@
     def state_copy(k):
         return remote(s_loc.at[oth0 + k], s_oth.at[k], s_ss.at[k], s_rs.at[k], core_peer, way)
 
-    def chip_copy(k):
-        return remote(c_tot.at[k], c_oth.at[k], c_ss.at[k], c_rs.at[k], x_peer, way)
-
-    def chain_copy(k):
+    def chip_copy(m):
+        return remote(c_tot.at[2 * m + 1 - x], c_oth.at[m], c_ss.at[m], c_rs.at[m], x_peer, way)
+
+    def chain_copy(m):
         up = lax.rem(me + GROUP, runs)
-        return remote(p_out.at[k], p_in.at[k], p_ss.at[k], p_rs.at[k], up, way)
+        return remote(p_out.at[m], p_in.at[m], p_ss.at[m], p_rs.at[m], up, way)
+
+    def return_copy(m):
+        return remote(g_out.at[m], g_in.at[m], g_ss.at[m], g_rs.at[m], x_peer, way)
 
     def carry_copy(k):
         return remote(e_send.at[k], e_oth.at[k], e_ss.at[k], e_rs.at[k], core_peer, way)
@@ -154,10 +156,11 @@
         state_copy(k).wait_recv()
         mine = power(rate, length * (1.0 - core_f))
         other = power(rate, length * core_f)
-        for p in range(CUTS):
-            rows = pl.ds(p * PIECE, PIECE)
-            c_tot[k * CUTS + p] = mine * s_loc[own0 + k, rows, :] + other * s_oth[k, rows, :]
-            chip_copy(k * CUTS + p).start()
+        c_tot[k] = mine * s_loc[own0 + k] + other * s_oth[k]
+
+        @pl.when(lax.rem(k, 2) != x)
+        def _():
+            chip_copy(k // 2).start()
 
     def state_step(k, c):
         local_states(k)
@@ -202,46 +205,53 @@
             )
             local[pair[n], pl.ds(b * BLOCK, BLOCK), :] = dot(jnp.concatenate([top, low], axis=0), vals, (1, 0))
 
-    def chain(s):
-        k = s // CUTS
-        rows = pl.ds(pl.multiple_of(lax.rem(s, CUTS) * PIECE, PIECE), PIECE)
+    def share(k, chip):
+        length_on = power(rates[own0 + k], float(length))
+
+        @pl.when(core == 0)
+        def _():
+            e_mine[k] = chip
+            e_send[k] = length_on * chip + s_loc[own0 + k]
+
+        @pl.when(core == 1)
+        def _():
+            e_mine[k] = length_on * chip + s_oth[k]
+            e_send[k] = chip
+
+        carry_copy(k).start()
+
+    def chain(m):
+        k = 2 * m + x
         rate = rates[own0 + k]
-        chip_copy(s).wait_recv()
+        chip_copy(m).wait_recv()
 
         @pl.when(z > 0)
         def _():
-            chain_copy(s).wait_recv()
-
-        before = p_in[s]
-        other = c_oth[s]
-        two = 2.0 * length
+            chain_copy(m).wait_recv()
+
+        before = p_in[m]
+        mine = c_tot[k]
+        other = c_oth[m]
+        chip_on = power(rate, 2.0 * length)
+        second = chip_on * before + ((1.0 - x_f) * mine + x_f * other)
 
         @pl.when(z < groups - 1)
         def _():
-            total = power(rate, two * (1.0 - x_f)) * c_tot[s] + power(rate, two * x_f) * other
-            p_out[s] = power(rate, 2.0 * two) * before + total
-            chain_copy(s).start()
-
-        chip = power(rate, two * x_f) * before + x_f * other
-
-        @pl.when(core == 0)
-        def _():
-            e_mine[s] = chip
-            e_send[s] = power(rate, float(length)) * chip + s_loc[own0 + k, rows, :]
-
-        @pl.when(core == 1)
-        def _():
-            e_mine[s] = power(rate, float(length)) * chip + s_oth[k, rows, :]
-            e_send[s] = chip
-
-        carry_copy(s).start()
+            p_out[m] = chip_on * second + (x_f * mine + (1.0 - x_f) * other)
+            chain_copy(m).start()
+
+        g_out[m] = x_f * before + (1.0 - x_f) * second
+        return_copy(m).start()
+        share(k, (1.0 - x_f) * before + x_f * second)
+
+    def relay(m):
+        return_copy(m).wait_recv()
+        share(2 * m + 1 - x, g_in[m])
 
     def finish(k):
         pair = (own0 + k, oth0 + k)
-        for p in range(CUTS):
-            carry_copy(k * CUTS + p).wait_recv()
-        parts = pl.ds(k * CUTS, CUTS)
-        carry = (e_mine[parts].reshape(E, E), e_oth[parts].reshape(E, E))
+        carry_copy(k).wait_recv()
+        carry = (e_mine[k], e_oth[k])
         scale = [rising(rates[h]) for h in pair]
         units = [(n, b) for b in range(blocks) for n in range(2)]
 
@@ -275,29 +285,25 @@
             attend(i)
 
         def turn(n, c):
-            k = 2 * (i - lag) + n
-            here = jnp.logical_and(k >= 0, k < half)
-
-            @pl.when(here)
+            m = 2 * (i - lag) + n
+
+            @pl.when(jnp.logical_and(m >= 0, m < quarter))
             def _():
-                chain(k * CUTS)
-
-            j = 2 * (i - top_lag) + n - 1
-
-            @pl.when(jnp.logical_and(j >= 0, j < half))
+                chain(m)
+
+            r = 2 * (i - top_lag) + n - 1
+
+            @pl.when(jnp.logical_and(r >= 0, r < quarter))
             def _():
-                finish(j)
-
-            @pl.when(here)
-            def _():
-                for p in range(1, CUTS):
-                    chain(k * CUTS + p)
+                relay(r)
+                finish(2 * r + x)
+                finish(2 * r + 1 - x)
 
             return c
 
         return lax.fori_loop(0, 2, turn, c)
 
-    lax.fori_loop(0, max(half, top_lag + (half + 1) // 2 + 1), step, 0)
+    lax.fori_loop(0, max(half, top_lag + (quarter + 1) // 2 + 1), step, 0)
 
     slabs = length // E
     for g in range(slabs):
@@ -313,17 +319,20 @@
 
     def drain(k, c):
         state_copy(k).wait_send()
-        for p in range(CUTS):
-            chip_copy(k * CUTS + p).wait_send()
-            carry_copy(k * CUTS + p).wait_send()
+        carry_copy(k).wait_send()
+        return c
+
+    def drain_links(m, c):
+        chip_copy(m).wait_send()
+        return_copy(m).wait_send()
 
         @pl.when(z < groups - 1)
         def _():
-            for p in range(CUTS):
-                chain_copy(k * CUTS + p).wait_send()
-
-        return c
-
+            chain_copy(m).wait_send()
+
+        return c
+
+    lax.fori_loop(0, quarter, drain_links, 0)
     lax.fori_loop(0, half, drain, 0)
     for d in range(1, ways):
         norm_copy(d).wait_send()
@@ -362,6 +371,7 @@
     length, columns = queries.shape
     heads = decay_rates.shape[0]
     half = heads // 2
+    quarter = half // 2
     blocks = length // BLOCK
     dma = pltpu.SemaphoreType.DMA
     states = [pltpu.VMEM((half, E, E), F32)]
@@ -383,12 +393,15 @@
             pltpu.VMEM((heads, E, E), F32),
         ]
         + states
-        + [pltpu.VMEM((half * CUTS, PIECE, E), F32)] * 7
+        + states
+        + [pltpu.VMEM((quarter, E, E), F32)] * 5
+        + states * 3
         + [pltpu.VMEM(sums_shape, F32), pltpu.VMEM((max(ways - 1, 1),) + sums_shape, F32)]
         + [dma]
         + [dma((heads,))] * 3
         + sems * 2
-        + [dma((half * CUTS,))] * 6
+        + [dma((quarter,))] * 6
+        + sems * 2
         + [dma((max(ways - 1, 1),))] * 2,
         compiler_params=pltpu.CompilerParams(
             collective_id=0, has_side_effects=True, vmem_limit_bytes=40 * 1024 * 1024

time: 35.6 us -> 36.4 us (1.022)
  Pallas kernels: 35.2 us -> 36.1 us
    pallas_call x1, Pallas kernels: 32 us -> 33 us  [body(): pl.pallas_call(functools.partial(kernel, runs, ways), out_shape=(jax.Shap...]
where the time goes in v1:
time: 36.4 us; the launch traced here: 36.1 us
  Pallas kernels  36.1 us (99%)
    pallas_call x1, Pallas kernels, body(): pl.pallas_call(functools.partial(kernel, runs, ways), out_shape=(jax.Shap...  33 us
    pallas_call x1, Pallas kernels, body(): pl.pallas_call(functools.partial(normalise, float(heads * ways * E)), out...  3.15 us

profile of v1, /device:TPU:24, one launch (start us, length us, event | category | flops | bytes accessed | tf_op | source)
XLA Modules:
  0.0 36.1 jit_solution(1823152536050912301)
XLA Ops:
  0.0 33.0 %shard_map.55 = (f32[16,1024,128]{2,1,0:T(8,128)S(1)}, f32[8,128]{1,0:T(8,128)S(1)}) custom-call(bf16[1024,2048]{1,0:T(8,128)(2,1)} %q_hbm.1, bf16[1024,2048]{1,0:T(8,128)(2,1)} %k_hbm.1, bf16[1024,2048]{1,0:T(8,128)(2,1)} %v_hbm.1, f32[16]{0:T(128)} %rates_hbm.1), custom_call_target="tpu_custom_call" | custom-call | flops 6442450944 | bytes 16777216 | tf_op jit(solution)/shard_map/pallas_call | solution.py:382
  33.0 3.2 %shard_map.56 = bf16[1024,2048]{1,0:T(8,128)(2,1)} custom-call(f32[16,1024,128]{2,1,0:T(8,128)S(1)} %get-tuple-element.7.mixed_ref, f32[8,128]{1,0:T(8,128)S(1)} %get-tuple-element.8.sums_ref, f32[1,2048]{1,0:T(1,128)} %bitcast.1), custom_call_target="tpu_custom_call" | custom-call | flops 6291456 | bytes 8388608 | tf_op jit(solution)/shard_map/pallas_call | solution.py:413

commit v2 on v1

--- a/solution.py
+++ b/solution.py
@@ -276,13 +276,10 @@
             if n == 1:
                 acc[rows, :] += squares
 
-    top_lag = half - 1
-    lag = jnp.where(z == groups - 1, top_lag, jnp.minimum(z, top_lag))
+    lag = jnp.minimum(2 * z, half - (quarter + 1) // 2)
 
     def step(i, c):
-        @pl.when(i < half)
-        def _():
-            attend(i)
+        attend(i)
 
         def turn(n, c):
             m = 2 * (i - lag) + n
@@ -291,19 +288,28 @@
             def _():
                 chain(m)
 
-            r = 2 * (i - top_lag) + n - 1
-
-            @pl.when(jnp.logical_and(r >= 0, r < quarter))
-            def _():
-                relay(r)
-                finish(2 * r + x)
-                finish(2 * r + 1 - x)
-
             return c
 
         return lax.fori_loop(0, 2, turn, c)
 
-    lax.fori_loop(0, max(half, top_lag + (quarter + 1) // 2 + 1), step, 0)
+    def owned(t, c):
+        @pl.when(t < quarter)
+        def _():
+            finish(2 * t + x)
+
+        @pl.when(t > 0)
+        def _():
+            relay(t - 1)
+
+        return c
+
+    def relayed(t, c):
+        finish(2 * t + 1 - x)
+        return c
+
+    lax.fori_loop(0, half, step, 0)
+    lax.fori_loop(0, quarter + 1, owned, 0)
+    lax.fori_loop(0, quarter, relayed, 0)
 
     slabs = length // E
     for g in range(slabs):

time: 36.4 us -> 33.7 us (0.926)
  Pallas kernels: 36.1 us -> 33.5 us
    pallas_call x1, Pallas kernels: 33 us -> 30.4 us  [body(): pl.pallas_call(functools.partial(kernel, runs, ways), out_shape=(jax.Shap...]
where the time goes in v2:
time: 33.7 us; the launch traced here: 33.5 us
  Pallas kernels  33.5 us (99%)
    pallas_call x1, Pallas kernels, body(): pl.pallas_call(functools.partial(kernel, runs, ways), out_shape=(jax.Shap...  30.4 us
    pallas_call x1, Pallas kernels, body(): pl.pallas_call(functools.partial(normalise, float(heads * ways * E)), out...  3.15 us

profile of v2, /device:TPU:24, one launch (start us, length us, event | category | flops | bytes accessed | tf_op | source)
XLA Modules:
  0.0 33.5 jit_solution(17681813102640419082)
XLA Ops:
  0.0 30.4 %shard_map.55 = (f32[16,1024,128]{2,1,0:T(8,128)S(1)}, f32[8,128]{1,0:T(8,128)S(1)}) custom-call(bf16[1024,2048]{1,0:T(8,128)(2,1)} %q_hbm.1, bf16[1024,2048]{1,0:T(8,128)(2,1)} %k_hbm.1, bf16[1024,2048]{1,0:T(8,128)(2,1)} %v_hbm.1, f32[16]{0:T(128)} %rates_hbm.1), custom_call_target="tpu_custom_call" | custom-call | flops 6442450944 | bytes 16777216 | tf_op jit(solution)/shard_map/pallas_call | solution.py:388
  30.4 3.2 %shard_map.56 = bf16[1024,2048]{1,0:T(8,128)(2,1)} custom-call(f32[16,1024,128]{2,1,0:T(8,128)S(1)} %get-tuple-element.7.mixed_ref, f32[8,128]{1,0:T(8,128)S(1)} %get-tuple-element.8.sums_ref, f32[1,2048]{1,0:T(1,128)} %bitcast.1), custom_call_target="tpu_custom_call" | custom-call | flops 6291456 | bytes 8388608 | tf_op jit(solution)/shard_map/pallas_call | solution.py:419

commit v3 on v2

--- a/solution.py
+++ b/solution.py
@@ -276,11 +276,9 @@
             if n == 1:
                 acc[rows, :] += squares
 
-    lag = jnp.minimum(2 * z, half - (quarter + 1) // 2)
+    lag = jnp.minimum(3 * z, half)
 
     def step(i, c):
-        attend(i)
-
         def turn(n, c):
             m = 2 * (i - lag) + n
 
@@ -290,10 +288,15 @@
 
             return c
 
-        return lax.fori_loop(0, 2, turn, c)
-
-    def owned(t, c):
-        @pl.when(t < quarter)
+        lax.fori_loop(0, 2, turn, 0)
+
+        @pl.when(i < half)
+        def _():
+            attend(i)
+
+        t = i - half
+
+        @pl.when(jnp.logical_and(t >= 0, t < quarter))
         def _():
             finish(2 * t + x)
 
@@ -307,8 +310,7 @@
         finish(2 * t + 1 - x)
         return c
 
-    lax.fori_loop(0, half, step, 0)
-    lax.fori_loop(0, quarter + 1, owned, 0)
+    lax.fori_loop(0, half + quarter + 1, step, 0)
     lax.fori_loop(0, quarter, relayed, 0)
 
     slabs = length // E

time: 33.7 us -> 33.6 us (level)
  no operation moved by 1% of the time
where the time goes in v3:
time: 33.6 us; the launch traced here: 33.4 us
  Pallas kernels  33.4 us (99%)
    pallas_call x1, Pallas kernels, body(): pl.pallas_call(functools.partial(kernel, runs, ways), out_shape=(jax.Shap...  30.2 us
    pallas_call x1, Pallas kernels, body(): pl.pallas_call(functools.partial(normalise, float(heads * ways * E)), out...  3.15 us

profile of v3, /device:TPU:24, one launch (start us, length us, event | category | flops | bytes accessed | tf_op | source)
XLA Modules:
  0.0 33.4 jit_solution(3243410612447130460)
XLA Ops:
  0.0 30.2 %shard_map.55 = (f32[16,1024,128]{2,1,0:T(8,128)S(1)}, f32[8,128]{1,0:T(8,128)S(1)}) custom-call(bf16[1024,2048]{1,0:T(8,128)(2,1)} %q_hbm.1, bf16[1024,2048]{1,0:T(8,128)(2,1)} %k_hbm.1, bf16[1024,2048]{1,0:T(8,128)(2,1)} %v_hbm.1, f32[16]{0:T(128)} %rates_hbm.1), custom_call_target="tpu_custom_call" | custom-call | flops 6442450944 | bytes 16777216 | tf_op jit(solution)/shard_map/pallas_call | solution.py:390
  30.2 3.2 %shard_map.56 = bf16[1024,2048]{1,0:T(8,128)(2,1)} custom-call(f32[16,1024,128]{2,1,0:T(8,128)S(1)} %get-tuple-element.7.mixed_ref, f32[8,128]{1,0:T(8,128)S(1)} %get-tuple-element.8.sums_ref, f32[1,2048]{1,0:T(1,128)} %bitcast.1), custom_call_target="tpu_custom_call" | custom-call | flops 6291456 | bytes 8388608 | tf_op jit(solution)/shard_map/pallas_call | solution.py:421
